TPU v7x, 32 devices: a whole 2x2x4 slice. The times are simulated.
32 devices in a mesh: groups: 2 (over y), row: 4 (over z), col: 2 (over x), sub: 2 (over core).
Axes of the slice: x: 2, y: 2, z: 4, core: 2. Of those that a mesh axis runs over, the one named last changes fastest.
Arguments:
- object_field: float32 [2, 4096, 512], P(None, ('groups', 'row', 'sub'), 'col'), parts along dimension 1, may hold values from -5 to 5
- probe_field: float32 [4, 256, 256], P('groups'), parts along dimension 0, may hold values from -5 to 5
- patterns: float32 [96, 256, 256], P(('groups', 'row', 'col', 'sub')), parts along dimension 0, may hold values from 0.1 to 3
- offset_rows: int32 [96], P(('groups', 'row', 'col', 'sub')), parts along dimension 0, may hold values from 0 to 1792, as said below
- offset_cols: int32 [96], P(('groups', 'row', 'col', 'sub')), parts along dimension 0, may hold values from 0 to 256, as said below
- counts: int32 [32], P(('groups', 'row', 'col', 'sub')), parts along dimension 0, may hold values from 1 to 3, as said below
- fresnel: float32 [1], replicated, may hold values from 0.05 to 0.5
- object_step: float32 [1], replicated, may hold values from 1 to 4
- probe_step: float32 [1], replicated, may hold values from 2 to 8
Outputs:
- object_out: float32 [2, 4096, 512], P(None, ('groups', 'row', 'sub'), 'col'), parts along dimension 1
- probe_out: float32 [4, 256, 256], P('groups'), parts along dimension 0
There are 2 independent parts, one for each index of `groups`. A program takes and returns all parts, laid end to end along the dimension named above; an argument that names none is the same for every part. Nothing has to cross between parts.
Inputs may be any that keep to these rules, and one draw needn't show every extreme that they name: `offset_rows`: position p belongs to owner p // 3, owners counted in the mesh order row, col, sub; its first row lies in that owner's object tile rows (tiles of 256 rows ordered by row, then sub) and its patch stays inside the object. `offset_cols`: its first column lies in the owner's tile columns (tiles of 256 columns ordered by col) and its patch stays inside the object. `counts`: an owner's live positions are its first slots.
All inputs are finite; a program needn't handle non-finite values.
Results may differ from a plain program's by a relative error of at most 0.0003.
Values sent between devices are 32-bit elements; how exact they have to be, the bound alone decides.
A program may use at most 64 MiB of HBM per device.

v0:
```python
import math

import jax
import jax.numpy as jnp
from jax import lax
from jax.sharding import PartitionSpec as P

ITERS = 2


HIGHEST = lax.Precision.HIGHEST


def shifted(value, axis, by):
    devices = lax.axis_size(axis)
    pairs = [(i, i + by) for i in range(devices) if 0 <= i + by < devices]
    return lax.ppermute(value, axis, pairs)


def propagator(fresnel, pixels):
    positions = jnp.arange(pixels, dtype=jnp.int32)
    product = positions[:, None] * positions[None, :] % pixels
    angles = 2.0 * math.pi / pixels * product.astype(jnp.float32)
    cosine = jnp.cos(angles)
    sine_table = jnp.sin(angles)
    frequency = jnp.where(positions < pixels // 2, positions, positions - pixels).astype(
        jnp.float32
    )
    phases = -math.pi / pixels * fresnel[0] * frequency * frequency
    trans_r = jnp.cos(phases)
    trans_i = jnp.sin(phases)
    left_r = (cosine * trans_r[None, :] - sine_table * trans_i[None, :]) / pixels
    left_i = (cosine * trans_i[None, :] + sine_table * trans_r[None, :]) / pixels
    kern_r = jnp.dot(left_r, cosine, precision=HIGHEST) + jnp.dot(
        left_i, sine_table, precision=HIGHEST
    )
    kern_i = jnp.dot(left_i, cosine, precision=HIGHEST) - jnp.dot(
        left_r, sine_table, precision=HIGHEST
    )
    return (kern_r, kern_i)


def apply_left(matrix, field):
    return jnp.einsum("mn,snk->smk", matrix, field, precision=HIGHEST)


def apply_right(field, matrix):
    return jnp.einsum("smn,nk->smk", field, matrix, precision=HIGHEST)


def propagate(kern_r, kern_i, field_r, field_i):
    middle_r = apply_left(kern_r, field_r) - apply_left(kern_i, field_i)
    middle_i = apply_left(kern_r, field_i) + apply_left(kern_i, field_r)
    out_r = apply_right(middle_r, kern_r) - apply_right(middle_i, kern_i)
    out_i = apply_right(middle_r, kern_i) + apply_right(middle_i, kern_r)
    return (out_r, out_i)


def local(
    object_field,
    probe_field,
    patterns,
    offset_rows,
    offset_cols,
    counts,
    fresnel,
    object_step,
    probe_step,
):
    pixels = probe_field.shape[1]
    tile_rows = object_field.shape[1]
    tile_cols = object_field.shape[2]
    slot_count = patterns.shape[0]
    kern_r, kern_i = propagator(fresnel, pixels)
    local_rows = offset_rows - lax.axis_index(("row", "sub")) * tile_rows
    local_cols = offset_cols - lax.axis_index("col") * tile_cols
    active = (jnp.arange(slot_count, dtype=jnp.int32) < counts[0]).astype(jnp.float32)
    for sweep_index in range(ITERS):
        right_cols = shifted(object_field, "col", -1)
        widened = jnp.concatenate([object_field, right_cols], axis=2)
        lower_rows = shifted(widened, ("row", "sub"), -1)
        region = jnp.concatenate([widened, lower_rows], axis=1)

        def cut_patch(row_at, col_at):
            return lax.dynamic_slice(region, (jnp.int32(0), row_at, col_at), (2, pixels, pixels))

        patches = jax.vmap(cut_patch)(local_rows, local_cols)
        obj_r = patches[:, 0]
        obj_i = patches[:, 1]
        probe_r = probe_field[0]
        probe_i = probe_field[1]
        exit_r = probe_r * obj_r - probe_i * obj_i
        exit_i = probe_r * obj_i + probe_i * obj_r
        wave_r, wave_i = propagate(kern_r, kern_i, exit_r, exit_i)
        excess = (wave_r * wave_r + wave_i * wave_i - patterns) * active[:, None, None]
        back_r, back_i = propagate(kern_r, -kern_i, excess * wave_r, excess * wave_i)
        probe_grad = jnp.stack(
            [
                jnp.sum(obj_r * back_r + obj_i * back_i, axis=0),
                jnp.sum(obj_r * back_i - obj_i * back_r, axis=0),
            ]
        )
        probe_weight = jnp.sum(active[:, None, None] * (obj_r * obj_r + obj_i * obj_i), axis=0)
        object_terms = jnp.stack(
            [probe_r * back_r + probe_i * back_i, probe_r * back_i - probe_i * back_r], axis=1
        )
        grad_region = jnp.zeros(region.shape, jnp.float32)
        for slot_index in range(slot_count):
            corner = (jnp.int32(0), local_rows[slot_index], local_cols[slot_index])
            existing = lax.dynamic_slice(grad_region, corner, (2, pixels, pixels))
            grad_region = lax.dynamic_update_slice(
                grad_region, existing + object_terms[slot_index], corner
            )
        spill_rows = shifted(grad_region[:, tile_rows:, :], ("row", "sub"), 1)
        grad_wide = grad_region[:, :tile_rows, :].at[:, :pixels, :].add(spill_rows)
        spill_cols = shifted(grad_wide[:, :, tile_cols:], "col", 1)
        grad_tile = grad_wide[:, :, :tile_cols].at[:, :, :pixels].add(spill_cols)
        largest = jnp.max(probe_r * probe_r + probe_i * probe_i)
        grad_total, weight_total = lax.psum((probe_grad, probe_weight), ("row", "col", "sub"))
        probe_next = probe_field - probe_step[0] * grad_total / (weight_total + 1.0)
        object_field = object_field - object_step[0] / (largest + 1e-06) * grad_tile
        probe_field = probe_next
    return (object_field, probe_field)


def solution(mesh):
    placed = (
        P(None, ("groups", "row", "sub"), "col"),
        P("groups", None, None),
        P(("groups", "row", "col", "sub"), None, None),
        P(("groups", "row", "col", "sub")),
        P(("groups", "row", "col", "sub")),
        P(("groups", "row", "col", "sub")),
        P(),
        P(),
        P(),
    )
    return jax.shard_map(
        local,
        mesh=mesh,
        in_specs=placed,
        out_specs=(P(None, ("groups", "row", "sub"), "col"), P("groups", None, None)),
        check_vma=False,
    )
```

profile of v0, /device:TPU:0, one launch (start us, length us, event | category | flops | bytes accessed | tf_op | source)
XLA Modules:
  0.0 416.6 jit_solution(7285951349452734700)
XLA Ops:
  11.7 1.5 fusion.73
  13.2 10.4 %collective-permute-done = f32[2,256,256]{2,1,0:T(8,128)S(1)} collective-permute-done((f32[2,256,256]{2,1,0:T(8,128)}, f32[2,256,256]{2,1,0:T(8,128)S(1)}, u32[]{:S(2)}, u32[]{:S(2)}) %collective-permute-start) | collective-permute-done | bytes 524320 | tf_op jit(solution)/shard_map/ppermute | solution.py:17
  37.6 1.5 fusion.8
  39.1 1.5 fusion.72
  40.6 1.5 convolution_subtract_fusion.8
  42.1 2.7 pad_maximum_fusion
  45.0 9.7 %while.10 = (s32[]{:T(128)}, f32[2,512,512]{2,1,0:T(8,128)}, s32[3,3]{1,0:T(4,128)S(1)}, f32[3,2,256,256]{3,2,0,1:T(8,128)S(1)}, s32[]{:T(128)}) while((s32[]{:T(128)}, f32[2,512,512]{2,1,0:T(8,128)}, s32[3,3]{1,0:T(4,128)S(1)}, f32[3,2,256,256]{3,2,0,1:T(8,128)S(1)}, s32[]{:T(128)}) %tuple.90), condition=%wide.while_cond.4, body=%wide.while_body.4.sunk | while | flops 2 | bytes 1048693 | solution.py:85
  45.6 2.6 bitcast_dynamic-update-slice_fusion.4
  48.8 2.6 bitcast_dynamic-update-slice_fusion.4
  51.9 2.6 bitcast_dynamic-update-slice_fusion.4
  56.1 1.4 fusion.132
  57.6 1.4 fusion.7
  61.8 1.4 fusion.6
  64.7 1.5 fusion.29
  66.2 1.8 fusion.155
  75.1 1.5 convolution_add_fusion.4
  76.6 2.7 fusion.21
  80.6 7.4 %dynamic_update_slice.18 = f32[2,512,512]{2,1,0:T(8,128)S(1)} dynamic-update-slice(f32[2,512,512]{2,1,0:T(8,128)S(1)} %broadcast.196.clone, f32[2,256,256]{2,1,0:T(8,128)} %fusion.40, s32[]{:T(128)} %constant.171.clone.1, s32[]{:T(128)S(6)} %select_n.78, s32[]{:T(128)S(6)} %select_n.79) | dynamic-update-slice | bytes 1048580 | tf_op jit(solution)/shard_map/dynamic_update_slice | solution.py:111
  88.0 2.0 fusion.38
  90.0 8.5 %dynamic_update_slice.19 = f32[2,512,512]{2,1,0:T(8,128)S(1)} dynamic-update-slice(f32[2,512,512]{2,1,0:T(8,128)S(1)} %dynamic_update_slice.18, f32[2,256,256]{2,1,0:T(8,128)} %fusion.38, s32[]{:T(128)} %constant.171.clone.1, s32[]{:T(128)S(6)} %select_n.80, s32[]{:T(128)S(6)} %select_n.81) | dynamic-update-slice | bytes 1048580 | tf_op jit(solution)/shard_map/dynamic_update_slice | solution.py:111
  98.5 2.0 fusion.48
  100.5 8.7 %dynamic_update_slice.20 = f32[2,512,512]{2,1,0:T(8,128)S(1)} dynamic-update-slice(f32[2,512,512]{2,1,0:T(8,128)S(1)} %dynamic_update_slice.19, f32[2,256,256]{2,1,0:T(8,128)} %fusion.48, s32[]{:T(128)} %constant.171.clone.1, s32[]{:T(128)S(6)} %select_n.82, s32[]{:T(128)S(6)} %select_n.83) | dynamic-update-slice | bytes 1048580 | tf_op jit(solution)/shard_map/dynamic_update_slice | solution.py:111
  109.2 5.0 %collective-permute-start.2 = (f32[2,256,512]{2,1,0:T(8,128)S(1)}, f32[2,256,512]{2,1,0:T(8,128)S(1)}, u32[]{:S(2)}, u32[]{:S(2)}) collective-permute-start(f32[2,256,512]{2,1,0:T(8,128)S(1)} %slice.229), channel_id=1, source_target_pairs={{0,1},{1,4},{4,5},{5,8},{8,9},{9,12},{12,13},{2,3},{3,6},{6,7},{7,... | collective-permute-start | bytes 3145736 | tf_op jit(solution)/shard_map/ppermute | solution.py:17
  114.3 2.2 collective-permute-done.2
  117.7 1.5 collective-permute-start.3
  121.2 4.6 %collective-permute-done.3 = f32[2,256,256]{2,1,0:T(8,128)S(1)} collective-permute-done((f32[2,256,256]{2,1,0:T(8,128)S(1)}, f32[2,256,256]{2,1,0:T(8,128)S(1)}, u32[]{:S(2)}, u32[]{:S(2)}) %collective-permute-start.3) | collective-permute-done | bytes 524320 | tf_op jit(solution)/shard_map/ppermute | solution.py:17
  129.2 8.9 %collective-permute-done.4 = f32[2,256,256]{2,1,0:T(8,128)S(1)} collective-permute-done((f32[2,256,256]{2,1,0:T(8,128)S(1)}, f32[2,256,256]{2,1,0:T(8,128)S(1)}, u32[]{:S(2)}, u32[]{:S(2)}) %collective-permute-start.4) | collective-permute-done | bytes 524320 | tf_op jit(solution)/shard_map/ppermute | solution.py:17
  141.2 96.3 %all-reduce.7.cloned.1.call-done = (f32[2,256,256]{2,1,0:T(8,128)}, f32[256,256]{1,0:T(8,128)}) async-done(((f32[2,256,256]{2,1,0:T(8,128)}, f32[256,256]{1,0:T(8,128)}), (f32[2,256,256]{2,1,0:T(8,128)}, f32[256,256]{1,0:T(8,128)})) %all-reduce.7.cloned.1.call-update) | async-done | bytes 786448 | tf_op jit(solution)/shard_map/psum | solution.py:119
  240.4 2.8 pad_maximum_fusion.1
  243.3 10.1 %while.11 = (s32[]{:T(128)}, f32[2,512,512]{2,1,0:T(8,128)}, s32[3,3]{1,0:T(4,128)S(1)}, f32[3,2,256,256]{3,2,0,1:T(8,128)S(1)}, s32[]{:T(128)}) while((s32[]{:T(128)}, f32[2,512,512]{2,1,0:T(8,128)}, s32[3,3]{1,0:T(4,128)S(1)}, f32[3,2,256,256]{3,2,0,1:T(8,128)S(1)}, s32[]{:T(128)}) %tuple.102), condition=%wide.while_cond.5, body=%wide.while_body.5.sunk | while | flops 2 | bytes 1048693 | solution.py:85
  244.0 2.6 bitcast_dynamic-update-slice_fusion.5
  247.3 2.6 bitcast_dynamic-update-slice_fusion.5
  250.6 2.6 bitcast_dynamic-update-slice_fusion.5
  254.8 1.4 fusion.142
  256.2 1.4 fusion.3
  260.5 1.4 fusion.2
  263.4 1.5 fusion.27
  264.9 1.6 fusion.159
  273.6 1.5 convolution_add_fusion
  275.1 2.7 fusion.12
  278.9 7.5 %dynamic_update_slice.21 = f32[2,512,512]{2,1,0:T(8,128)S(1)} dynamic-update-slice(f32[2,512,512]{2,1,0:T(8,128)S(1)} %broadcast.196, f32[2,256,256]{2,1,0:T(8,128)S(1)} %fusion.35, s32[]{:T(128)} %constant.171.clone.1, s32[]{:T(128)S(6)} %select_n.78, s32[]{:T(128)S(6)} %select_n.79) | dynamic-update-slice | bytes 1048580 | tf_op jit(solution)/shard_map/dynamic_update_slice | solution.py:111
  287.7 9.5 %dynamic_update_slice.22 = f32[2,512,512]{2,1,0:T(8,128)S(1)} dynamic-update-slice(f32[2,512,512]{2,1,0:T(8,128)S(1)} %dynamic_update_slice.21, f32[2,256,256]{2,1,0:T(8,128)S(1)} %fusion.33, s32[]{:T(128)} %constant.171.clone.1, s32[]{:T(128)S(6)} %select_n.80, s32[]{:T(128)S(6)} %select_n.81) | dynamic-update-slice | bytes 1048580 | tf_op jit(solution)/shard_map/dynamic_update_slice | solution.py:111
  298.3 9.6 %dynamic_update_slice.23 = f32[2,512,512]{2,1,0:T(8,128)S(1)} dynamic-update-slice(f32[2,512,512]{2,1,0:T(8,128)S(1)} %dynamic_update_slice.22, f32[2,256,256]{2,1,0:T(8,128)S(1)} %fusion.44, s32[]{:T(128)} %constant.171.clone.1, s32[]{:T(128)S(6)} %select_n.82, s32[]{:T(128)S(6)} %select_n.83) | dynamic-update-slice | bytes 1048580 | tf_op jit(solution)/shard_map/dynamic_update_slice | solution.py:111
  309.0 4.4 %collective-permute-start.6 = (f32[2,256,512]{2,1,0:T(8,128)}, f32[2,256,512]{2,1,0:T(8,128)}, u32[]{:S(2)}, u32[]{:S(2)}) collective-permute-start(f32[2,256,512]{2,1,0:T(8,128)} %slice.239), channel_id=1, source_target_pairs={{0,1},{1,4},{4,5},{5,8},{8,9},{9,12},{12,13},{2,3},{3,6},{6,7},{7,... | collective-permute-start | bytes 3145736 | tf_op jit(solution)/shard_map/ppermute | solution.py:17
  315.0 1.4 slice_add_fusion
  318.3 1.4 collective-permute-start.7
  321.1 84.6 %all-reduce.5.cloned.1.call-done = (f32[2,256,256]{2,1,0:T(8,128)}, f32[256,256]{1,0:T(8,128)}) async-done(((f32[2,256,256]{2,1,0:T(8,128)}, f32[256,256]{1,0:T(8,128)}), (f32[2,256,256]{2,1,0:T(8,128)}, f32[256,256]{1,0:T(8,128)})) %all-reduce.5.cloned.1.call-update) | async-done | bytes 786448 | tf_op jit(solution)/shard_map/psum | solution.py:119
  406.6 1.9 divide_subtract_fusion
  (113 shorter events, 57.8 us)
Async XLA Ops:
  7.2 230.3 %all-reduce.7.cloned.1.call-start = ((), (), s32[]{:S(2)}) async-start(), calls=%async_computation.1 | async-start | bytes 1572864 | tf_op jit(solution)/shard_map/psum | solution.py:119
  7.2 16.4 %collective-permute-start = (f32[2,256,256]{2,1,0:T(8,128)}, f32[2,256,256]{2,1,0:T(8,128)S(1)}, u32[]{:S(2)}, u32[]{:S(2)}) collective-permute-start(f32[2,256,256]{2,1,0:T(8,128)} %param.25), channel_id=1, source_target_pairs={{2,0},{3,1},{6,4},{7,5},{10,8},{11,9},{14,12},{15,13},{18,16},{19,... | collective-permute-start | bytes 1572872 | tf_op jit(solution)/shard_map/ppermute | solution.py:17
  23.7 18.4 %collective-permute-start.1 = (f32[2,256,512]{2,1,0:T(8,128)S(1)}, f32[2,256,512]{2,1,0:T(8,128)}, u32[]{:S(2)}, u32[]{:S(2)}) collective-permute-start(f32[2,256,512]{2,1,0:T(8,128)S(1)} %constant_dynamic-update-slice_fusion), channel_id=1, source_target_pairs={{1,0},{4,1},{5,4},{8,5},{9,8},{12,9},{13,12},{3,2},{6,3},{7,6},{10... | collective-permute-start | bytes 3145736 | tf_op jit(solution)/shard_map/ppermute | solution.py:17
  40.5 1.5 copy-start.6
  63.2 1.4 copy-start.11
  79.3 1.1 copy-start.1
  109.2 10.6 %copy-start.7 = (f32[2,256,256]{2,1,0:T(8,128)S(1)}, f32[2,256,256]{2,1,0:T(8,128)}, u32[]{:S(2)}) copy-start(f32[2,256,256]{2,1,0:T(8,128)} %param.26) | copy-start | bytes 1572868
  109.2 7.2 %collective-permute-start.2 = (f32[2,256,512]{2,1,0:T(8,128)S(1)}, f32[2,256,512]{2,1,0:T(8,128)S(1)}, u32[]{:S(2)}, u32[]{:S(2)}) collective-permute-start(f32[2,256,512]{2,1,0:T(8,128)S(1)} %slice.229), channel_id=1, source_target_pairs={{0,1},{1,4},{4,5},{5,8},{8,9},{9,12},{12,13},{2,3},{3,6},{6,7},{7,... | collective-permute-start | bytes 3145736 | tf_op jit(solution)/shard_map/ppermute | solution.py:17
  116.7 1.0 copy-start.10
  117.7 8.2 %copy-start.13 = (f32[2,256,256]{2,1,0:T(8,128)S(1)}, f32[2,256,256]{2,1,0:T(8,128)}, u32[]{:S(2)}) copy-start(f32[2,256,256]{2,1,0:T(8,128)} %param.25) | copy-start | bytes 1572868
  117.7 10.6 %copy-start.14 = (f32[256,256]{1,0:T(8,128)S(1)}, f32[256,256]{1,0:T(8,128)}, u32[]{:S(2)}) copy-start(f32[256,256]{1,0:T(8,128)} %get-tuple-element.108) | copy-start | bytes 786436
  117.7 10.6 %copy-start.15 = (f32[256,256]{1,0:T(8,128)S(1)}, f32[256,256]{1,0:T(8,128)}, u32[]{:S(2)}) copy-start(f32[256,256]{1,0:T(8,128)} %get-tuple-element.109) | copy-start | bytes 786436
  117.7 8.1 %collective-permute-start.3 = (f32[2,256,256]{2,1,0:T(8,128)S(1)}, f32[2,256,256]{2,1,0:T(8,128)S(1)}, u32[]{:S(2)}, u32[]{:S(2)}) collective-permute-start(f32[2,256,256]{2,1,0:T(8,128)S(1)} %slice.231), channel_id=1, source_target_pairs={{0,2},{1,3},{4,6},{5,7},{8,10},{9,11},{12,14},{13,15},{16,18},{17,... | collective-permute-start | bytes 1572872 | tf_op jit(solution)/shard_map/ppermute | solution.py:17
  127.0 112.7 %copy-start.2 = (f32[2,256,256]{2,1,0:T(8,128)}, f32[2,256,256]{2,1,0:T(8,128)S(1)}, u32[]{:S(2)}) copy-start(f32[2,256,256]{2,1,0:T(8,128)S(1)} %fusion.46) | copy-start | bytes 1572868
  127.0 11.1 %collective-permute-start.4 = (f32[2,256,256]{2,1,0:T(8,128)S(1)}, f32[2,256,256]{2,1,0:T(8,128)S(1)}, u32[]{:S(2)}, u32[]{:S(2)}) collective-permute-start(f32[2,256,256]{2,1,0:T(8,128)S(1)} %fusion.46), channel_id=1, source_target_pairs={{2,0},{3,1},{6,4},{7,5},{10,8},{11,9},{14,12},{15,13},{18,16},{19,... | collective-permute-start | bytes 1572872 | tf_op jit(solution)/shard_map/ppermute | solution.py:17
  129.2 276.5 %all-reduce.5.cloned.1.call-start = ((), (), s32[]{:S(2)}) async-start(), calls=%async_computation | async-start | bytes 1572864 | tf_op jit(solution)/shard_map/psum | solution.py:119
  139.2 100.4 %collective-permute-start.5 = (f32[2,256,512]{2,1,0:T(8,128)}, f32[2,256,512]{2,1,0:T(8,128)}, u32[]{:S(2)}, u32[]{:S(2)}) collective-permute-start(f32[2,256,512]{2,1,0:T(8,128)} %pad_maximum_fusion.2), channel_id=1, source_target_pairs={{1,0},{4,1},{5,4},{8,5},{9,8},{12,9},{13,12},{3,2},{6,3},{7,6},{10... | collective-permute-start | bytes 3145736 | tf_op jit(solution)/shard_map/ppermute | solution.py:17
  239.6 0.8 copy-start.4
  261.9 1.4 copy-start.12
  277.8 0.9 copy-start
  298.3 15.1 %copy-start.16 = (f32[256,256]{1,0:T(8,128)S(1)}, f32[256,256]{1,0:T(8,128)}, u32[]{:S(2)}) copy-start(f32[256,256]{1,0:T(8,128)} %get-tuple-element.106) | copy-start | bytes 786436
  298.3 15.1 %copy-start.17 = (f32[256,256]{1,0:T(8,128)S(1)}, f32[256,256]{1,0:T(8,128)}, u32[]{:S(2)}) copy-start(f32[256,256]{1,0:T(8,128)} %get-tuple-element.107) | copy-start | bytes 786436
  309.0 6.0 %collective-permute-start.6 = (f32[2,256,512]{2,1,0:T(8,128)}, f32[2,256,512]{2,1,0:T(8,128)}, u32[]{:S(2)}, u32[]{:S(2)}) collective-permute-start(f32[2,256,512]{2,1,0:T(8,128)} %slice.239), channel_id=1, source_target_pairs={{0,1},{1,4},{4,5},{5,8},{8,9},{9,12},{12,13},{2,3},{3,6},{6,7},{7,... | collective-permute-start | bytes 3145736 | tf_op jit(solution)/shard_map/ppermute | solution.py:17
  314.2 5.5 %copy-start.5 = (f32[2,256,256]{2,1,0:T(8,128)S(1)}, f32[2,256,256]{2,1,0:T(8,128)}, u32[]{:S(2)}) copy-start(f32[2,256,256]{2,1,0:T(8,128)} %copy-done.4) | copy-start | bytes 1572868
  316.4 1.0 copy-start.8
  318.3 90.3 %copy-start.3 = (f32[2,256,256]{2,1,0:T(8,128)S(1)}, f32[2,256,256]{2,1,0:T(8,128)}, u32[]{:S(2)}) copy-start(f32[2,256,256]{2,1,0:T(8,128)} %copy-done.2) | copy-start | bytes 1572868
  318.3 90.3 %copy-start.9 = (f32[2,256,512]{2,1,0:T(8,128)S(1)}, f32[2,256,512]{2,1,0:T(8,128)}, u32[]{:S(2)}) copy-start(f32[2,256,512]{2,1,0:T(8,128)} %copy-done.8) | copy-start | bytes 3145732
  318.3 90.3 %collective-permute-start.7 = (f32[2,256,256]{2,1,0:T(8,128)}, f32[2,256,256]{2,1,0:T(8,128)S(1)}, u32[]{:S(2)}, u32[]{:S(2)}) collective-permute-start(f32[2,256,256]{2,1,0:T(8,128)} %slice.241), channel_id=1, source_target_pairs={{0,2},{1,3},{4,6},{5,7},{8,10},{9,11},{12,14},{13,15},{16,18},{17,... | collective-permute-start | bytes 1572872 | tf_op jit(solution)/shard_map/ppermute | solution.py:17
Sparse Core Ops, SparseCore 0:
  129.3 108.1 all-reduce.6
  314.3 91.2 all-reduce.4
where the time goes:
time: 424 us; the launch traced here: 417 us
  waiting for transfers between devices  208 us (49%)
  local copies, waits for them, and re-layouts  79.6 us (19%)
  matrix products  54.6 us (13%)
  between operations  30.3 us (7%)
  other arithmetic  26.3 us (6%)
  starting transfers between devices  17.5 us (4%)
    psum x2, waiting for transfers between devices, local(): lax.psum((probe_grad, probe_weight), ('row', 'col', 'sub'))  181 us
    dynamic_update_slice x6, local copies, waits for them, and re-layouts, local(): lax.dynamic_update_slice(grad_region, existing + object_terms[slot_index]...  51.2 us
    ppermute x8, waiting for transfers between devices, shifted(): return lax.ppermute(value, axis, pairs)  26.9 us
    dot_general x16, matrix products, apply_right(): return jnp.einsum('smn,nk->smk', field, matrix, precision=HIGHEST)  25.5 us
    dot_general x16, matrix products, apply_left(): return jnp.einsum('mn,snk->smk', matrix, field, precision=HIGHEST)  23.2 us
    gather x18, local copies, waits for them, and re-layouts  19.3 us
    ppermute x8, starting transfers between devices, shifted(): return lax.ppermute(value, axis, pairs)  17.5 us
  transfers between devices with their start and end apart: 10, of which 7 were waited for; matrix products, arithmetic and copies ran while one was open for 5% of the time, Pallas kernels for 0%

commit v1 on v0

v1 whole, which is shorter than its diff:
```python
import functools
import math

import jax
import jax.numpy as jnp
import numpy as np
from jax import lax
from jax.experimental import pallas as pl
from jax.experimental.pallas import tpu as pltpu
from jax.sharding import PartitionSpec as P

ITERS = 2
CHUNKS = 4
HIGHEST = lax.Precision.HIGHEST
MESH = pl.DeviceIdType.MESH


def split(value):
    high = value.astype(jnp.bfloat16)
    return high, (value - high.astype(jnp.float32)).astype(jnp.bfloat16)


def build_propagator(n, fresnel_ref, cosine_ref, sine_ref, left_ref, right_ref):
    freq = lax.broadcasted_iota(jnp.int32, (8, n), 1)
    freq = jnp.where(freq < n // 2, freq, freq - n).astype(jnp.float32)
    phases = -math.pi / n * fresnel_ref[0] * freq * freq
    trans_r = jnp.cos(phases)[0:1]
    trans_i = jnp.sin(phases)[0:1]
    cosine = cosine_ref[...]
    sine = sine_ref[...]
    half_r = (cosine * trans_r - sine * trans_i) * (1.0 / n)
    half_i = (cosine * trans_i + sine * trans_r) * (1.0 / n)

    def exact(a, b):
        return jnp.dot(a, b, precision=HIGHEST, preferred_element_type=jnp.float32)

    kern_r = exact(half_r, cosine) + exact(half_i, sine)
    kern_i = exact(half_i, cosine) - exact(half_r, sine)
    r_high, r_low = split(kern_r)
    i_high, i_low = split(kern_i)
    for part, (r_half, i_half) in enumerate(((r_high, i_high), (r_low, i_low), (r_high, i_high))):
        base = part * 2 * n
        left_ref[:n, base : base + n] = r_half
        left_ref[:n, base + n : base + 2 * n] = -i_half
        left_ref[n:, base : base + n] = i_half
        left_ref[n:, base + n : base + 2 * n] = r_half
        right_ref[base : base + n, :n] = r_half
        right_ref[base : base + n, n:] = i_half
        right_ref[base + n : base + 2 * n, :n] = -i_half
        right_ref[base + n : base + 2 * n, n:] = r_half


def gradients(
    sizes,
    rows_ref,
    cols_ref,
    counts_ref,
    region,
    probe,
    patterns_ref,
    left_ref,
    right_ref,
    grad,
    partial,
    padded,
    stacked,
    patch_ref,
):
    n_sub = sizes[2]
    slots, n = patterns_ref.shape[0], patterns_ref.shape[1]
    tile = lax.axis_index("row") * n_sub + lax.axis_index("sub")
    col = lax.axis_index("col")

    def propagate(x_r, x_i):
        for k, value in enumerate((x_r, x_i)):
            high, low = split(value)
            stacked[k * n : (k + 1) * n, :] = high
            stacked[(k + 2) * n : (k + 3) * n, :] = high
            stacked[(k + 4) * n : (k + 5) * n, :] = low
        mid = jnp.dot(left_ref[...], stacked[...], preferred_element_type=jnp.float32)
        a_high, a_low = split(mid[:n])
        b_high, b_low = split(mid[n:])
        wide = jnp.concatenate([a_high, b_high, a_high, b_high, a_low, b_low], axis=1)
        out = jnp.dot(wide, right_ref[...], preferred_element_type=jnp.float32)
        return out[:, :n], out[:, n:]

    padded[:, :n, :] = jnp.zeros((2, n, 2 * n), jnp.float32)
    padded[:, 2 * n :, :] = jnp.zeros((2, n, 2 * n), jnp.float32)
    grad[...] = jnp.zeros(grad.shape, jnp.float32)
    partial[...] = jnp.zeros(partial.shape, jnp.float32)

    def visit(p, carry):
        row_at = rows_ref[p] - tile * n
        col_at = cols_ref[p] - col * n
        shift = lax.rem(2 * n - col_at, 2 * n)
        alive = jnp.where(p < counts_ref[0], 1.0, 0.0).astype(jnp.float32)
        aligned = pl.multiple_of(row_at // 8 * 8, 8)
        inner = row_at % 8
        sublane = lax.broadcasted_iota(jnp.int32, (1, 8, 2 * n), 1)
        for k in range(2):
            rows = region[k, pl.ds(aligned, n + 8), :].reshape(n // 8 + 1, 8, 2 * n)
            rows = pltpu.roll(rows, lax.rem(8 - inner, 8), 1)
            rows = jnp.where(sublane < 8 - inner, rows[:-1], rows[1:]).reshape(n, 2 * n)
            patch_ref[k] = pltpu.roll(rows, shift, 1)[:, :n]
        obj_r, obj_i = patch_ref[0], patch_ref[1]
        probe_r, probe_i = probe[0], probe[1]
        wave_r, wave_i = propagate(
            probe_r * obj_r - probe_i * obj_i, probe_r * obj_i + probe_i * obj_r
        )
        excess = (wave_r * wave_r + wave_i * wave_i - patterns_ref[p]) * alive
        back_r, back_m = propagate(excess * wave_r, -(excess * wave_i))
        obj_r, obj_i = patch_ref[0], patch_ref[1]
        probe_r, probe_i = probe[0], probe[1]
        partial[0] += obj_r * back_r - obj_i * back_m
        partial[1] += -(obj_r * back_m) - obj_i * back_r
        partial[2] += alive * (obj_r * obj_r + obj_i * obj_i)
        terms = (probe_r * back_r - probe_i * back_m, -(probe_r * back_m) - probe_i * back_r)
        for k in range(2):
            wide = jnp.concatenate([terms[k], jnp.zeros((n, n), jnp.float32)], axis=1)
            wide = pltpu.roll(wide, col_at, 1).reshape(n // 8, 8, 2 * n)
            wide = pltpu.roll(wide, inner, 1)
            empty = jnp.zeros((1, 8, 2 * n), jnp.float32)
            after, before = jnp.concatenate([wide, empty], 0), jnp.concatenate([empty, wide], 0)
            wide = jnp.where(sublane < inner, before, after).reshape(n + 8, 2 * n)
            padded[k, n : 2 * n + 8, :] = wide
            grad[k] += padded[k, pl.ds(pl.multiple_of(n - aligned, 8), 2 * n), :]
        return carry

    lax.fori_loop(0, slots, visit, 0)


def exchange_first(
    sizes, fresnel_ref, object_ref, cosine_ref, sine_ref, region, left_ref, right_ref, halo_send, halo_recv
):
    n_row, n_col, n_sub = sizes
    n = region.shape[1] // 2
    step_rows = n // CHUNKS
    row, col, sub = lax.axis_index("row"), lax.axis_index("col"), lax.axis_index("sub")
    tile = row * n_sub + sub
    n_tile = n_row * n_sub
    has_up, has_down = tile > 0, tile < n_tile - 1
    has_left, has_right = col > 0, col < n_col - 1
    up = {"row": (tile + n_tile - 1) % n_tile // n_sub, "sub": (tile + n_tile - 1) % n_tile % n_sub}
    down = {"row": (tile + 1) % n_tile // n_sub, "sub": (tile + 1) % n_tile % n_sub}
    left = {"col": (col + n_col - 1) % n_col}
    right = {"col": (col + 1) % n_col}

    barrier = pltpu.get_barrier_semaphore()

    def greet(where):
        pl.semaphore_signal(barrier, inc=1, device_id=where, device_id_type=MESH)

    for d in range(1, n_row):
        greet({"row": (row + d) % n_row})
    for d in range(1, n_col):
        greet({"col": (col + d) % n_col})
    for d in range(1, n_sub):
        greet({"sub": (sub + d) % n_sub})
    cross_up = (sub == 0) & (row > 0)
    cross_down = (sub == n_sub - 1) & (row < n_row - 1)
    pl.when(cross_up)(lambda: greet(up))
    pl.when(cross_down)(lambda: greet(down))
    crossing = cross_up.astype(jnp.int32) + cross_down.astype(jnp.int32)
    pl.semaphore_wait(barrier, n_row + n_col + n_sub - 3 + crossing)

    def remote(src, dst, send, recv, where):
        return pltpu.make_async_remote_copy(
            src_ref=src, dst_ref=dst, send_sem=send, recv_sem=recv, device_id=where, device_id_type=MESH
        )

    def halo(kind, q):
        at = pl.ds(q * step_rows, step_rows)
        below = pl.ds(n + q * step_rows, step_rows)
        own, far = pl.ds(0, n), pl.ds(n, n)
        src, dst, where = (
            (region.at[:, at, own], region.at[:, at, far], left),
            (region.at[:, at, own], region.at[:, below, own], up),
            (region.at[:, at, far], region.at[:, below, far], up),
        )[kind]
        return remote(src, dst, halo_send.at[kind, q], halo_recv.at[kind, q], where)

    halo_out = (has_left, has_up, has_up & has_right)
    halo_in = (has_right, has_down, has_down & has_right)

    def when_start(cond, copy):
        pl.when(cond)(lambda: copy.start())

    def when_recv(cond, copy):
        pl.when(cond)(lambda: copy.wait_recv())

    def clear_edges():
        @pl.when(~has_right)
        def _():
            region[:, :, n:] = jnp.zeros((2, 2 * n, n), jnp.float32)

        @pl.when(~has_down)
        def _():
            region[:, n:, :] = jnp.zeros((2, n, 2 * n), jnp.float32)

    clear_edges()
    region[:, :n, :n] = object_ref[...]
    for q in range(CHUNKS):
        when_start(halo_out[0], halo(0, q))
        when_start(halo_out[1], halo(1, q))
    build_propagator(n, fresnel_ref, cosine_ref, sine_ref, left_ref, right_ref)
    for q in range(CHUNKS):
        when_recv(halo_in[0], halo(0, q))
        when_start(halo_out[2], halo(2, q))
    for q in range(CHUNKS):
        when_recv(halo_in[1], halo(1, q))
        when_recv(halo_in[2], halo(2, q))
    for q in range(CHUNKS):
        for kind in range(3):
            pl.when(halo_out[kind])(lambda copy=halo(kind, q): copy.wait_send())


def exchange_next(
    sizes,
    last,
    object_step_ref,
    probe_step_ref,
    old_region,
    probe,
    grad,
    partial,
    target,
    probe_next,
    far_sum,
    own_sum,
    total,
    from_up,
    from_corner,
    from_left,
    from_sub,
    from_col,
    from_row,
    halo_send,
    halo_recv,
    spill_send,
    spill_recv,
    sub_send,
    sub_recv,
    col_send,
    col_recv,
    row_send,
    row_recv,
):
    region = target if not last else old_region
    n_row, n_col, n_sub = sizes
    n = region.shape[1] // 2
    step_rows = n // CHUNKS
    row, col, sub = lax.axis_index("row"), lax.axis_index("col"), lax.axis_index("sub")
    tile = row * n_sub + sub
    n_tile = n_row * n_sub
    has_up, has_down = tile > 0, tile < n_tile - 1
    has_left, has_right = col > 0, col < n_col - 1
    up = {"row": (tile + n_tile - 1) % n_tile // n_sub, "sub": (tile + n_tile - 1) % n_tile % n_sub}
    down = {"row": (tile + 1) % n_tile // n_sub, "sub": (tile + 1) % n_tile % n_sub}
    left = {"col": (col + n_col - 1) % n_col}
    right = {"col": (col + 1) % n_col}

    barrier = pltpu.get_barrier_semaphore()

    def greet(where):
        pl.semaphore_signal(barrier, inc=1, device_id=where, device_id_type=MESH)

    for d in range(1, n_row):
        greet({"row": (row + d) % n_row})
    for d in range(1, n_col):
        greet({"col": (col + d) % n_col})
    for d in range(1, n_sub):
        greet({"sub": (sub + d) % n_sub})
    cross_up = (sub == 0) & (row > 0)
    cross_down = (sub == n_sub - 1) & (row < n_row - 1)
    pl.when(cross_up)(lambda: greet(up))
    pl.when(cross_down)(lambda: greet(down))
    crossing = cross_up.astype(jnp.int32) + cross_down.astype(jnp.int32)
    pl.semaphore_wait(barrier, n_row + n_col + n_sub - 3 + crossing)

    def remote(src, dst, send, recv, where):
        return pltpu.make_async_remote_copy(
            src_ref=src, dst_ref=dst, send_sem=send, recv_sem=recv, device_id=where, device_id_type=MESH
        )

    def halo(kind, q):
        at = pl.ds(q * step_rows, step_rows)
        below = pl.ds(n + q * step_rows, step_rows)
        own, far = pl.ds(0, n), pl.ds(n, n)
        src, dst, where = (
            (region.at[:, at, own], region.at[:, at, far], left),
            (region.at[:, at, own], region.at[:, below, own], up),
            (region.at[:, at, far], region.at[:, below, far], up),
        )[kind]
        return remote(src, dst, halo_send.at[kind, q], halo_recv.at[kind, q], where)

    halo_out = (has_left, has_up, has_up & has_right)
    halo_in = (has_right, has_down, has_down & has_right)

    def spill(kind, q):
        at = pl.ds(q * step_rows, step_rows)
        below = pl.ds(n + q * step_rows, step_rows)
        own, far = pl.ds(0, n), pl.ds(n, n)
        src, dst, where = (
            (far_sum.at[:, at, :], from_left.at[:, at, :], right),
            (grad.at[:, below, own], from_up.at[:, at, :], down),
            (grad.at[:, below, far], from_corner.at[:, at, :], down),
        )[kind]
        return remote(src, dst, spill_send.at[kind, q], spill_recv.at[kind, q], where)

    spill_out = (has_right, has_down, has_down & has_right)
    spill_in = (has_left, has_up, has_up & has_right)

    def when_start(cond, copy):
        pl.when(cond)(lambda: copy.start())

    def when_recv(cond, copy):
        pl.when(cond)(lambda: copy.wait_recv())

    def clear_edges():
        @pl.when(~has_right)
        def _():
            region[:, :, n:] = jnp.zeros((2, 2 * n, n), jnp.float32)

        @pl.when(~has_down)
        def _():
            region[:, n:, :] = jnp.zeros((2, n, 2 * n), jnp.float32)

    sub_rows = n // n_sub
    col_rows = sub_rows // n_col
    pieces = min(n_row, col_rows // 8)
    row_rows = col_rows // pieces
    sub_base = sub * sub_rows
    col_base = sub_base + col * col_rows
    row_base = col_base + row * row_rows
    owns = row < pieces

    def span(start, length):
        return pl.ds(pl.multiple_of(start, 8), length)

    def scatter_sub(d):
        to = (sub + d) % n_sub
        return remote(
            partial.at[:, span(to * sub_rows, sub_rows), :], from_sub.at[d - 1],
            sub_send.at[0, d - 1], sub_recv.at[0, d - 1], {"sub": to},
        )

    def scatter_col(d):
        to = (col + d) % n_col
        return remote(
            total.at[:, span(to * col_rows, col_rows), :], from_col.at[d - 1],
            col_send.at[0, d - 1], col_recv.at[0, d - 1], {"col": to},
        )

    def scatter_row(d):
        to = (row + d) % n_row
        return remote(
            total.at[:, span(col * col_rows + jnp.minimum(to, pieces - 1) * row_rows, row_rows), :],
            from_row.at[d - 1],
            row_send.at[0, d - 1], row_recv.at[0, d - 1], {"row": to},
        )

    def gather(axis, d):
        me, count, base, length, send, recv = {
            "row": (row, n_row, row_base, row_rows, row_send, row_recv),
            "col": (col, n_col, col_base, col_rows, col_send, col_recv),
            "sub": (sub, n_sub, sub_base, sub_rows, sub_send, sub_recv),
        }[axis]
        part = probe_next.at[:, span(base, length), :]
        return remote(part, part, send.at[1, d - 1], recv.at[1, d - 1], {axis: (me + d) % count})

    for d in range(1, n_sub):
        scatter_sub(d).start()
    for q in range(CHUNKS):
        when_start(spill_out[2], spill(2, q))
    for q in range(CHUNKS):
        when_start(spill_out[1], spill(1, q))
    if not last:
        clear_edges()
    far_sum[...] = grad[:, :n, n:]
    own_sum[...] = grad[:, :n, :n]
    peak = probe[0] * probe[0] + probe[1] * probe[1]
    peak = jnp.max(jnp.max(peak, axis=0, keepdims=True), axis=1, keepdims=True)
    scale = object_step_ref[0] / (peak + 1e-6)

    total[...] = partial[:, span(sub_base, sub_rows), :]
    for d in range(1, n_sub):
        scatter_sub(d).wait_recv()
        total[...] += from_sub[d - 1]
    for d in range(1, n_col):
        scatter_col(d).start()

    for q in range(CHUNKS):
        at = slice(q * step_rows, (q + 1) * step_rows)

        @pl.when(spill_in[2])
        def _():
            spill(2, q).wait_recv()
            far_sum[:, at, :] += from_corner[:, at, :]

        when_start(spill_out[0], spill(0, q))

    mine = span(col * col_rows, col_rows)
    for d in range(1, n_col):
        scatter_col(d).wait_recv()
        total[:, mine, :] += from_col[d - 1]
    for d in range(1, n_row):
        copy = scatter_row(d)
        if pieces == n_row:
            copy.start()
        else:
            when_start((row + d) % n_row < pieces, copy)

    for q in range(CHUNKS):
        at = slice(q * step_rows, (q + 1) * step_rows)

        @pl.when(spill_in[1])
        def _():
            spill(1, q).wait_recv()
            own_sum[:, at, :] += from_up[:, at, :]

        @pl.when(spill_in[0])
        def _():
            spill(0, q).wait_recv()
            own_sum[:, at, :] += from_left[:, at, :]

        fresh = old_region[:, at, :n] - scale * own_sum[:, at, :]
        if last:
            target[:, at, :] = fresh
        else:
            region[:, at, :n] = fresh
            when_start(halo_out[0], halo(0, q))
            when_start(halo_out[1], halo(1, q))

    def finish_piece():
        mine = span(row_base, row_rows)
        sums = total[:, span(col * col_rows + row * row_rows, row_rows), :]
        for d in range(1, n_row):
            scatter_row(d).wait_recv()
            sums = sums + from_row[d - 1]
        for k in range(2):
            probe_next[k, mine, :] = probe[k, mine, :] - probe_step_ref[0] * sums[k] / (sums[2] + 1.0)
        for d in range(1, n_row):
            gather("row", d).start()

    if pieces == n_row:
        finish_piece()
    else:
        pl.when(owns)(finish_piece)
    if not last:
        for q in range(CHUNKS):
            when_recv(halo_in[0], halo(0, q))
            when_start(halo_out[2], halo(2, q))
    for d in range(1, n_row):
        copy = gather("row", d)
        if pieces == n_row:
            copy.wait_recv()
        else:
            when_recv((row + n_row - d) % n_row < pieces, copy)
    for axis, count in (("col", n_col), ("sub", n_sub)):
        for d in range(1, count):
            gather(axis, d).start()
        for d in range(1, count):
            gather(axis, d).wait_recv()
    if not last:
        for q in range(CHUNKS):
            when_recv(halo_in[1], halo(1, q))
            when_recv(halo_in[2], halo(2, q))

    for q in range(CHUNKS):
        for kind in range(3):
            pl.when(spill_out[kind])(lambda copy=spill(kind, q): copy.wait_send())
            if not last:
                pl.when(halo_out[kind])(lambda copy=halo(kind, q): copy.wait_send())
    for d in range(1, n_sub):
        scatter_sub(d).wait_send()
        gather("sub", d).wait_send()
    for d in range(1, n_col):
        scatter_col(d).wait_send()
        gather("col", d).wait_send()
    for d in range(1, n_row):
        for cond, copy in (((row + d) % n_row < pieces, scatter_row(d)), (owns, gather("row", d))):
            if pieces == n_row:
                copy.wait_send()
            else:
                pl.when(cond)(lambda copy=copy: copy.wait_send())


def solution(mesh):
    n_row, n_col, n_sub = mesh.shape["row"], mesh.shape["col"], mesh.shape["sub"]

    def local(
        object_field, probe_field, patterns, offset_rows, offset_cols, counts, fresnel, object_step, probe_step
    ):
        n = probe_field.shape[1]
        index = np.arange(n)
        angles = 2.0 * np.pi / n * (index[:, None] * index[None, :] % n)
        cosine = np.cos(angles).astype(np.float32)
        sine = np.sin(angles).astype(np.float32)
        sub_rows = n // n_sub
        col_rows = sub_rows // n_col
        row_rows = col_rows // min(n_row, col_rows // 8)
        f32 = jnp.float32
        dma = pltpu.SemaphoreType.DMA
        smem = pl.BlockSpec(memory_space=pltpu.SMEM)
        vmem = pl.BlockSpec(memory_space=pltpu.VMEM)
        sizes = (n_row, n_col, n_sub)
        region_shape = jax.ShapeDtypeStruct((2, 2 * n, 2 * n), f32)
        tile_shape = jax.ShapeDtypeStruct((2, n, n), f32)
        tile_scratch = pltpu.VMEM((2, n, n), f32)
        limit = 24 * 1024 * 1024
        copies = [dma((3, CHUNKS)), dma((3, CHUNKS))]

        region, left, right = pl.pallas_call(
            functools.partial(exchange_first, sizes),
            out_shape=(
                region_shape,
                jax.ShapeDtypeStruct((2 * n, 6 * n), jnp.bfloat16),
                jax.ShapeDtypeStruct((6 * n, 2 * n), jnp.bfloat16),
            ),
            in_specs=[smem, vmem, vmem, vmem],
            out_specs=(vmem, vmem, vmem),
            scratch_shapes=copies,
            compiler_params=pltpu.CompilerParams(
                collective_id=0, has_side_effects=True, vmem_limit_bytes=limit
            ),
        )(fresnel, object_field, jnp.asarray(cosine), jnp.asarray(sine))

        probe = probe_field
        for it in range(ITERS):
            last = it == ITERS - 1
            grad, partial = pl.pallas_call(
                functools.partial(gradients, sizes),
                out_shape=(region_shape, jax.ShapeDtypeStruct((3, n, n), f32)),
                in_specs=[smem] * 3 + [vmem] * 5,
                out_specs=(vmem, vmem),
                scratch_shapes=[
                    pltpu.VMEM((2, 3 * n, 2 * n), f32),
                    pltpu.VMEM((6 * n, n), jnp.bfloat16),
                    tile_scratch,
                ],
                compiler_params=pltpu.CompilerParams(vmem_limit_bytes=limit),
            )(offset_rows, offset_cols, counts, region, probe, patterns, left, right)
            region, probe = pl.pallas_call(
                functools.partial(exchange_next, sizes, last),
                out_shape=(tile_shape if last else region_shape, tile_shape),
                in_specs=[smem] * 2 + [vmem] * 4,
                out_specs=(vmem, vmem),
                scratch_shapes=[
                    tile_scratch,
                    tile_scratch,
                    pltpu.VMEM((3, sub_rows, n), f32),
                    tile_scratch,
                    tile_scratch,
                    tile_scratch,
                    pltpu.VMEM((n_sub - 1, 3, sub_rows, n), f32),
                    pltpu.VMEM((n_col - 1, 3, col_rows, n), f32),
                    pltpu.VMEM((n_row - 1, 3, row_rows, n), f32),
                ]
                + copies
                + copies
                + [dma((2, count - 1)) for count in (n_sub, n_sub, n_col, n_col, n_row, n_row)],
                compiler_params=pltpu.CompilerParams(
                    collective_id=1 + it, has_side_effects=True, vmem_limit_bytes=limit
                ),
            )(object_step, probe_step, region, probe, grad, partial)
        return region, probe

    owners = ("groups", "row", "col", "sub")
    tiled = P(None, ("groups", "row", "sub"), "col")
    probes = P("groups", None, None)
    return jax.shard_map(
        local,
        mesh=mesh,
        in_specs=(tiled, probes, P(owners, None, None), P(owners), P(owners), P(owners), P(), P(), P()),
        out_specs=(tiled, probes),
        check_vma=False,
    )
```

time: 424 us -> 124 us (0.29); the launches traced: 417 us -> 124 us
  waiting for transfers between devices: 208 us -> 0 us
  Pallas kernels: 0 us -> 112 us
  local copies, waits for them, and re-layouts: 79.6 us -> 8.02 us
  matrix products: 54.6 us -> 0 us
  between operations: 30.3 us -> 3.33 us
  other arithmetic: 26.3 us -> 0 us
  starting transfers between devices: 17.5 us -> 0 us
    psum x2 -> x0, waiting for transfers between devices: 181 us -> none  [local(): lax.psum((probe_grad, probe_weight), ('row', 'col', 'sub'))]
    pallas_call x0 -> x5, Pallas kernels: none -> 112 us  [the longest x2 65.8 us: local(): pl.pallas_call(functools.partial(exchange_next, sizes, last), out_shape=(...]
    dot_general x36 -> x0, matrix products: 54.6 us -> none  [the longest x16 25.5 us: apply_right(): return jnp.einsum('smn,nk->smk', field, matrix, precision=HIGHEST)]
    dynamic_update_slice x6 -> x0, local copies, waits for them, and re-layouts: 51.2 us -> none  [local(): lax.dynamic_update_slice(grad_region, existing + object_terms[slot_index]...]
    ppermute x8 -> x0, waiting for transfers between devices: 26.9 us -> none  [shifted(): return lax.ppermute(value, axis, pairs)]
    gather x18 -> x0, local copies, waits for them, and re-layouts: 19.3 us -> none
    ppermute x8 -> x0, starting transfers between devices: 17.5 us -> none  [shifted(): return lax.ppermute(value, axis, pairs)]
    add x8 -> x0, other arithmetic: 9.82 us -> none  [the longest x4 6.25 us: local(): existing + object_terms[slot_index]]
  transfers between devices with their start and end apart: 10 -> 0, of which waited for: 7 -> 0; matrix products, arithmetic and copies ran while one was open for 5% -> 0% of each run, Pallas kernels for 0% -> 0%
where the time goes in v1:
time: 124 us
  Pallas kernels  112 us (90%)
  local copies, waits for them, and re-layouts  8.02 us (6%)
  between operations  3.33 us (3%)
    pallas_call x2, Pallas kernels, local(): pl.pallas_call(functools.partial(exchange_next, sizes, last), out_shape=(...  65.8 us
    pallas_call x2, Pallas kernels, local(): pl.pallas_call(functools.partial(gradients, sizes), out_shape=(region_sha...  28.1 us
    pallas_call x1, Pallas kernels, local(): pl.pallas_call(functools.partial(exchange_first, sizes), out_shape=(regio...  18.5 us
    unnamed x24, local copies, waits for them, and re-layouts  8.02 us

profile of v1, /device:TPU:0, one launch (start us, length us, event | category | flops | bytes accessed | tf_op | source)
XLA Modules:
  0.0 123.8 jit_solution(9201274878570205820)
XLA Ops:
  3.2 0.0 copy-start.4
  3.2 1.0 copy-done.4
  4.3 0.0 copy-start.5
  4.3 0.9 copy-done.5
  5.2 0.0 copy-start.6
  5.2 0.9 copy-done.6
  6.2 18.5 %shard_map.122 = (f32[2,512,512]{2,1,0:T(8,128)S(1)}, bf16[512,1536]{1,0:T(8,128)(2,1)S(1)}, bf16[1536,512]{1,0:T(8,128)(2,1)S(1)}) custom-call(f32[1]{0:T(128)S(6)} %copy.16.fresnel_ref, f32[2,256,256]{2,1,0:T(8,128)S(1)} %copy-done.4, f32[256,256]{1,0:T(8,128)S(1)} %copy-done.6, f32[256,256]{1,0:T(8,128)S(1)} %copy-done.5), custom_call_target="tpu_custom_call" | custom-call | tf_op jit(solution)/shard_map/pallas_call | solution.py:513
  24.7 0.0 copy-start
  24.7 1.1 copy-done
  25.8 0.0 copy-start.2
  25.8 1.0 copy-done.2
  26.9 0.0 copy-start.7
  26.9 0.7 copy-done.7
  27.5 0.0 copy-start.9
  27.5 0.7 copy-done.9
  28.2 0.0 copy-start.3
  28.2 14.1 %shard_map.123 = (f32[2,512,512]{2,1,0:T(8,128)S(1)}, f32[3,256,256]{2,1,0:T(8,128)S(1)}) custom-call(s32[3]{0:T(128)S(1)} %copy-done.7, s32[3]{0:T(128)S(1)} %copy-done.9, s32[1]{0:T(128)S(6)} %copy.15.counts_ref, f32[2,512,512]{2,1,0:T(8,128)S(1)} %get-tuple-element.11.region.old_region, f32[2,256,256]{2,1,0:T(8,128)S(1)} %copy-done.2, ...), custom_call_target="tpu_custom_call" | custom-call | tf_op jit(solution)/shard_map/pallas_call | solution.py:531
  42.3 0.0 copy-done.3
  42.3 0.0 copy-start.1
  42.3 0.0 copy-start.8
  42.4 0.0 copy-start.10
  42.4 35.0 %shard_map.124 = (f32[2,512,512]{2,1,0:T(8,128)S(1)}, f32[2,256,256]{2,1,0:T(8,128)S(1)}) custom-call(f32[1]{0:T(128)S(6)} %copy.17.object_step_ref, f32[1]{0:T(128)S(6)} %copy.18.probe_step_ref, f32[2,512,512]{2,1,0:T(8,128)S(1)} %get-tuple-element.11.region.old_region, f32[2,256,256]{2,1,0:T(8,128)S(1)} %copy-done.3, ...), custom_call_target="tpu_custom_call" | custom-call | tf_op jit(solution)/shard_map/pallas_call | solution.py:543
  77.4 0.0 copy-done.1
  77.4 0.0 copy-done.8
  77.4 0.0 copy-done.10
  77.4 14.0 %shard_map.125 = (f32[2,512,512]{2,1,0:T(8,128)S(1)}, f32[3,256,256]{2,1,0:T(8,128)S(1)}) custom-call(s32[3]{0:T(128)S(1)} %copy-done.8, s32[3]{0:T(128)S(1)} %copy-done.10, s32[1]{0:T(128)S(6)} %copy.15.counts_ref, f32[2,512,512]{2,1,0:T(8,128)S(1)} %get-tuple-element.16.region.old_region, f32[2,256,256]{2,1,0:T(8,128)S(1)} %get-tuple-element.17.probe, ...), custom_call_target="tpu_custom_call" | custom-call | tf_op jit(solution)/shard_map/pallas_call | solution.py:531
  91.4 30.8 %shard_map.126 = (f32[2,256,256]{2,1,0:T(8,128)S(1)}, f32[2,256,256]{2,1,0:T(8,128)S(1)}) custom-call(f32[1]{0:T(128)S(6)} %copy.17.object_step_ref, f32[1]{0:T(128)S(6)} %copy.18.probe_step_ref, f32[2,512,512]{2,1,0:T(8,128)S(1)} %get-tuple-element.16.region.old_region, f32[2,256,256]{2,1,0:T(8,128)S(1)} %get-tuple-element.17.probe, ...), custom_call_target="tpu_custom_call" | custom-call | tf_op jit(solution)/shard_map/pallas_call | solution.py:543
  122.2 0.8 copy.19
  123.0 0.8 copy.20
Async XLA Ops:
  3.2 1.0 copy-start.4
  4.3 0.9 copy-start.5
  5.2 0.9 copy-start.6
  24.7 1.1 copy-start
  25.8 1.0 copy-start.2
  26.9 0.7 copy-start.7
  27.5 0.7 copy-start.9
  28.2 14.2 %copy-start.3 = (f32[2,256,256]{2,1,0:T(8,128)S(1)}, f32[2,256,256]{2,1,0:T(8,128)}, u32[]{:S(2)}) copy-start(f32[2,256,256]{2,1,0:T(8,128)} %probe.3) | copy-start | bytes 1572868
  42.3 35.0 %copy-start.1 = (f32[3,256,256]{2,1,0:T(8,128)S(1)}, f32[3,256,256]{2,1,0:T(8,128)}, u32[]{:S(2)}) copy-start(f32[3,256,256]{2,1,0:T(8,128)} %patterns_ref.3) | copy-start | bytes 2359300
  42.3 35.0 %copy-start.8 = (s32[3]{0:T(128)S(1)}, s32[3]{0:T(128)}, u32[]{:S(2)}) copy-start(s32[3]{0:T(128)} %rows_ref.3) | copy-start | bytes 40
  42.4 35.0 %copy-start.10 = (s32[3]{0:T(128)S(1)}, s32[3]{0:T(128)}, u32[]{:S(2)}) copy-start(s32[3]{0:T(128)} %cols_ref.3) | copy-start | bytes 40

commit v2 on v1

--- a/solution.py
+++ b/solution.py
@@ -3,7 +3,6 @@
 
 import jax
 import jax.numpy as jnp
-import numpy as np
 from jax import lax
 from jax.experimental import pallas as pl
 from jax.experimental.pallas import tpu as pltpu
@@ -11,6 +10,7 @@
 
 ITERS = 2
 CHUNKS = 4
+HALVES = 2
 HIGHEST = lax.Precision.HIGHEST
 MESH = pl.DeviceIdType.MESH
 
@@ -20,14 +20,16 @@
     return high, (value - high.astype(jnp.float32)).astype(jnp.bfloat16)
 
 
-def build_propagator(n, fresnel_ref, cosine_ref, sine_ref, left_ref, right_ref):
+def build_propagator(n, fresnel_ref, left_ref, right_ref):
     freq = lax.broadcasted_iota(jnp.int32, (8, n), 1)
     freq = jnp.where(freq < n // 2, freq, freq - n).astype(jnp.float32)
     phases = -math.pi / n * fresnel_ref[0] * freq * freq
     trans_r = jnp.cos(phases)[0:1]
     trans_i = jnp.sin(phases)[0:1]
-    cosine = cosine_ref[...]
-    sine = sine_ref[...]
+    product = lax.broadcasted_iota(jnp.int32, (n, n), 0) * lax.broadcasted_iota(jnp.int32, (n, n), 1)
+    angles = 2.0 * math.pi / n * lax.rem(product, n).astype(jnp.float32)
+    cosine = jnp.cos(angles)
+    sine = jnp.sin(angles)
     half_r = (cosine * trans_r - sine * trans_i) * (1.0 / n)
     half_i = (cosine * trans_i + sine * trans_r) * (1.0 / n)
 
@@ -44,10 +46,8 @@
         left_ref[:n, base + n : base + 2 * n] = -i_half
         left_ref[n:, base : base + n] = i_half
         left_ref[n:, base + n : base + 2 * n] = r_half
-        right_ref[base : base + n, :n] = r_half
-        right_ref[base : base + n, n:] = i_half
-        right_ref[base + n : base + 2 * n, :n] = -i_half
-        right_ref[base + n : base + 2 * n, n:] = r_half
+        right_ref[part * n : (part + 1) * n, :n] = r_half
+        right_ref[part * n : (part + 1) * n, n:] = i_half
 
 
 def gradients(
@@ -71,25 +71,24 @@
     tile = lax.axis_index("row") * n_sub + lax.axis_index("sub")
     col = lax.axis_index("col")
 
-    def propagate(x_r, x_i):
+    def propagate(stacked, x_r, x_i):
         for k, value in enumerate((x_r, x_i)):
             high, low = split(value)
             stacked[k * n : (k + 1) * n, :] = high
             stacked[(k + 2) * n : (k + 3) * n, :] = high
             stacked[(k + 4) * n : (k + 5) * n, :] = low
         mid = jnp.dot(left_ref[...], stacked[...], preferred_element_type=jnp.float32)
-        a_high, a_low = split(mid[:n])
-        b_high, b_low = split(mid[n:])
-        wide = jnp.concatenate([a_high, b_high, a_high, b_high, a_low, b_low], axis=1)
+        high, low = split(mid)
+        wide = jnp.concatenate([high, high, low], axis=1)
         out = jnp.dot(wide, right_ref[...], preferred_element_type=jnp.float32)
-        return out[:, :n], out[:, n:]
-
-    padded[:, :n, :] = jnp.zeros((2, n, 2 * n), jnp.float32)
-    padded[:, 2 * n :, :] = jnp.zeros((2, n, 2 * n), jnp.float32)
+        return out[:n, :n] - out[n:, n:], out[:n, n:] + out[n:, :n]
+
+    padded[:, :n, :] = jnp.zeros((padded.shape[0], n, 2 * n), jnp.float32)
+    padded[:, 2 * n :, :] = jnp.zeros((padded.shape[0], n, 2 * n), jnp.float32)
     grad[...] = jnp.zeros(grad.shape, jnp.float32)
     partial[...] = jnp.zeros(partial.shape, jnp.float32)
 
-    def visit(p, carry):
+    def visit(p):
         row_at = rows_ref[p] - tile * n
         col_at = cols_ref[p] - col * n
         shift = lax.rem(2 * n - col_at, 2 * n)
@@ -101,15 +100,15 @@
             rows = region[k, pl.ds(aligned, n + 8), :].reshape(n // 8 + 1, 8, 2 * n)
             rows = pltpu.roll(rows, lax.rem(8 - inner, 8), 1)
             rows = jnp.where(sublane < 8 - inner, rows[:-1], rows[1:]).reshape(n, 2 * n)
-            patch_ref[k] = pltpu.roll(rows, shift, 1)[:, :n]
-        obj_r, obj_i = patch_ref[0], patch_ref[1]
+            patch_ref[2 * p + k] = pltpu.roll(rows, shift, 1)[:, :n]
+        obj_r, obj_i = patch_ref[2 * p], patch_ref[2 * p + 1]
         probe_r, probe_i = probe[0], probe[1]
         wave_r, wave_i = propagate(
-            probe_r * obj_r - probe_i * obj_i, probe_r * obj_i + probe_i * obj_r
+            stacked.at[2 * p], probe_r * obj_r - probe_i * obj_i, probe_r * obj_i + probe_i * obj_r
         )
         excess = (wave_r * wave_r + wave_i * wave_i - patterns_ref[p]) * alive
-        back_r, back_m = propagate(excess * wave_r, -(excess * wave_i))
-        obj_r, obj_i = patch_ref[0], patch_ref[1]
+        back_r, back_m = propagate(stacked.at[2 * p + 1], excess * wave_r, -(excess * wave_i))
+        obj_r, obj_i = patch_ref[2 * p], patch_ref[2 * p + 1]
         probe_r, probe_i = probe[0], probe[1]
         partial[0] += obj_r * back_r - obj_i * back_m
         partial[1] += -(obj_r * back_m) - obj_i * back_r
@@ -122,15 +121,15 @@
             empty = jnp.zeros((1, 8, 2 * n), jnp.float32)
             after, before = jnp.concatenate([wide, empty], 0), jnp.concatenate([empty, wide], 0)
             wide = jnp.where(sublane < inner, before, after).reshape(n + 8, 2 * n)
-            padded[k, n : 2 * n + 8, :] = wide
-            grad[k] += padded[k, pl.ds(pl.multiple_of(n - aligned, 8), 2 * n), :]
-        return carry
-
-    lax.fori_loop(0, slots, visit, 0)
+            padded[2 * p + k, n : 2 * n + 8, :] = wide
+            grad[k] += padded[2 * p + k, pl.ds(pl.multiple_of(n - aligned, 8), 2 * n), :]
+
+    for p in range(slots):
+        visit(p)
 
 
 def exchange_first(
-    sizes, fresnel_ref, object_ref, cosine_ref, sine_ref, region, left_ref, right_ref, halo_send, halo_recv
+    sizes, fresnel_ref, object_ref, region, left_ref, right_ref, halo_send, halo_recv
 ):
     n_row, n_col, n_sub = sizes
     n = region.shape[1] // 2
@@ -197,12 +196,12 @@
         def _():
             region[:, n:, :] = jnp.zeros((2, n, 2 * n), jnp.float32)
 
-    clear_edges()
     region[:, :n, :n] = object_ref[...]
     for q in range(CHUNKS):
         when_start(halo_out[0], halo(0, q))
         when_start(halo_out[1], halo(1, q))
-    build_propagator(n, fresnel_ref, cosine_ref, sine_ref, left_ref, right_ref)
+    clear_edges()
+    build_propagator(n, fresnel_ref, left_ref, right_ref)
     for q in range(CHUNKS):
         when_recv(halo_in[0], halo(0, q))
         when_start(halo_out[2], halo(2, q))
@@ -325,71 +324,75 @@
         def _():
             region[:, n:, :] = jnp.zeros((2, n, 2 * n), jnp.float32)
 
-    sub_rows = n // n_sub
+    sub_rows = n // HALVES // n_sub
     col_rows = sub_rows // n_col
     pieces = min(n_row, col_rows // 8)
     row_rows = col_rows // pieces
-    sub_base = sub * sub_rows
-    col_base = sub_base + col * col_rows
-    row_base = col_base + row * row_rows
+    sub_base = [h * (n // HALVES) + sub * sub_rows for h in range(HALVES)]
+    col_base = [base + col * col_rows for base in sub_base]
+    row_base = [base + row * row_rows for base in col_base]
     owns = row < pieces
 
     def span(start, length):
         return pl.ds(pl.multiple_of(start, 8), length)
 
-    def scatter_sub(d):
+    def scatter_sub(h, d):
         to = (sub + d) % n_sub
         return remote(
-            partial.at[:, span(to * sub_rows, sub_rows), :], from_sub.at[d - 1],
-            sub_send.at[0, d - 1], sub_recv.at[0, d - 1], {"sub": to},
+            partial.at[:, span(h * (n // HALVES) + to * sub_rows, sub_rows), :], from_sub.at[h, d - 1],
+            sub_send.at[h, 0, d - 1], sub_recv.at[h, 0, d - 1], {"sub": to},
         )
 
-    def scatter_col(d):
+    def scatter_col(h, d):
         to = (col + d) % n_col
         return remote(
-            total.at[:, span(to * col_rows, col_rows), :], from_col.at[d - 1],
-            col_send.at[0, d - 1], col_recv.at[0, d - 1], {"col": to},
+            total.at[h, :, span(to * col_rows, col_rows), :], from_col.at[h, d - 1],
+            col_send.at[h, 0, d - 1], col_recv.at[h, 0, d - 1], {"col": to},
         )
 
-    def scatter_row(d):
+    def scatter_row(h, d):
         to = (row + d) % n_row
         return remote(
-            total.at[:, span(col * col_rows + jnp.minimum(to, pieces - 1) * row_rows, row_rows), :],
-            from_row.at[d - 1],
-            row_send.at[0, d - 1], row_recv.at[0, d - 1], {"row": to},
+            total.at[h, :, span(col * col_rows + jnp.minimum(to, pieces - 1) * row_rows, row_rows), :],
+            from_row.at[h, d - 1],
+            row_send.at[h, 0, d - 1], row_recv.at[h, 0, d - 1], {"row": to},
         )
 
-    def gather(axis, d):
+    def gather(h, axis, d):
         me, count, base, length, send, recv = {
-            "row": (row, n_row, row_base, row_rows, row_send, row_recv),
-            "col": (col, n_col, col_base, col_rows, col_send, col_recv),
-            "sub": (sub, n_sub, sub_base, sub_rows, sub_send, sub_recv),
+            "row": (row, n_row, row_base[h], row_rows, row_send, row_recv),
+            "col": (col, n_col, col_base[h], col_rows, col_send, col_recv),
+            "sub": (sub, n_sub, sub_base[h], sub_rows, sub_send, sub_recv),
         }[axis]
         part = probe_next.at[:, span(base, length), :]
-        return remote(part, part, send.at[1, d - 1], recv.at[1, d - 1], {axis: (me + d) % count})
-
-    for d in range(1, n_sub):
-        scatter_sub(d).start()
+        return remote(part, part, send.at[h, 1, d - 1], recv.at[h, 1, d - 1], {axis: (me + d) % count})
+
+    halves = range(HALVES)
+    for h in halves:
+        for d in range(1, n_sub):
+            scatter_sub(h, d).start()
     for q in range(CHUNKS):
         when_start(spill_out[2], spill(2, q))
-    for q in range(CHUNKS):
+    far_sum[...] = grad[:, :n, n:]
+    mine = span(col * col_rows, col_rows)
+    for h in halves:
+        total[h] = partial[:, span(sub_base[h], sub_rows), :]
+        for d in range(1, n_sub):
+            scatter_sub(h, d).wait_recv()
+            total[h] += from_sub[h, d - 1]
+        for d in range(1, n_col):
+            scatter_col(h, d).start()
+    ahead = 1 if last else CHUNKS
+    for q in range(ahead):
         when_start(spill_out[1], spill(1, q))
+    own_sum[...] = grad[:, :n, :n]
     if not last:
         clear_edges()
-    far_sum[...] = grad[:, :n, n:]
-    own_sum[...] = grad[:, :n, :n]
     peak = probe[0] * probe[0] + probe[1] * probe[1]
     peak = jnp.max(jnp.max(peak, axis=0, keepdims=True), axis=1, keepdims=True)
     scale = object_step_ref[0] / (peak + 1e-6)
 
-    total[...] = partial[:, span(sub_base, sub_rows), :]
-    for d in range(1, n_sub):
-        scatter_sub(d).wait_recv()
-        total[...] += from_sub[d - 1]
-    for d in range(1, n_col):
-        scatter_col(d).start()
-
-    for q in range(CHUNKS):
+    def pass_right(q):
         at = slice(q * step_rows, (q + 1) * step_rows)
 
         @pl.when(spill_in[2])
@@ -399,18 +402,34 @@
 
         when_start(spill_out[0], spill(0, q))
 
-    mine = span(col * col_rows, col_rows)
-    for d in range(1, n_col):
-        scatter_col(d).wait_recv()
-        total[:, mine, :] += from_col[d - 1]
-    for d in range(1, n_row):
-        copy = scatter_row(d)
-        if pieces == n_row:
-            copy.start()
-        else:
-            when_start((row + d) % n_row < pieces, copy)
-
-    for q in range(CHUNKS):
+    for h in halves:
+        for d in range(1, n_col):
+            scatter_col(h, d).wait_recv()
+            total[h, :, mine, :] += from_col[h, d - 1]
+        for d in range(1, n_row):
+            copy = scatter_row(h, d)
+            if pieces == n_row:
+                copy.start()
+            else:
+                when_start((row + d) % n_row < pieces, copy)
+        pass_right(h)
+    for q in range(ahead, CHUNKS):
+        when_start(spill_out[1], spill(1, q))
+    for q in range(HALVES, CHUNKS):
+        pass_right(q)
+
+    def finish_piece(h):
+        mine = span(row_base[h], row_rows)
+        sums = total[h, :, span(col * col_rows + row * row_rows, row_rows), :]
+        for d in range(1, n_row):
+            scatter_row(h, d).wait_recv()
+            sums = sums + from_row[h, d - 1]
+        for k in range(2):
+            probe_next[k, mine, :] = probe[k, mine, :] - probe_step_ref[0] * sums[k] / (sums[2] + 1.0)
+        for d in range(1, n_row):
+            gather(h, "row", d).start()
+
+    def update(q):
         at = slice(q * step_rows, (q + 1) * step_rows)
 
         @pl.when(spill_in[1])
@@ -431,36 +450,38 @@
             when_start(halo_out[0], halo(0, q))
             when_start(halo_out[1], halo(1, q))
 
-    def finish_piece():
-        mine = span(row_base, row_rows)
-        sums = total[:, span(col * col_rows + row * row_rows, row_rows), :]
+    if not last:
+        for q in range(HALVES):
+            update(q)
+    for h in halves:
+        if pieces == n_row:
+            finish_piece(h)
+        else:
+            pl.when(owns)(functools.partial(finish_piece, h))
+    for h in halves:
         for d in range(1, n_row):
-            scatter_row(d).wait_recv()
-            sums = sums + from_row[d - 1]
-        for k in range(2):
-            probe_next[k, mine, :] = probe[k, mine, :] - probe_step_ref[0] * sums[k] / (sums[2] + 1.0)
-        for d in range(1, n_row):
-            gather("row", d).start()
-
-    if pieces == n_row:
-        finish_piece()
-    else:
-        pl.when(owns)(finish_piece)
+            copy = gather(h, "row", d)
+            if pieces == n_row:
+                copy.wait_recv()
+            else:
+                when_recv((row + n_row - d) % n_row < pieces, copy)
+        for d in range(1, n_col):
+            gather(h, "col", d).start()
+        update(h if last else HALVES + h)
+    for h in halves:
+        for d in range(1, n_col):
+            gather(h, "col", d).wait_recv()
+        for d in range(1, n_sub):
+            gather(h, "sub", d).start()
+    for q in range(HALVES if last else 2 * HALVES, CHUNKS):
+        update(q)
     if not last:
         for q in range(CHUNKS):
             when_recv(halo_in[0], halo(0, q))
             when_start(halo_out[2], halo(2, q))
-    for d in range(1, n_row):
-        copy = gather("row", d)
-        if pieces == n_row:
-            copy.wait_recv()
-        else:
-            when_recv((row + n_row - d) % n_row < pieces, copy)
-    for axis, count in (("col", n_col), ("sub", n_sub)):
-        for d in range(1, count):
-            gather(axis, d).start()
-        for d in range(1, count):
-            gather(axis, d).wait_recv()
+    for h in halves:
+        for d in range(1, n_sub):
+            gather(h, "sub", d).wait_recv()
     if not last:
         for q in range(CHUNKS):
             when_recv(halo_in[1], halo(1, q))
@@ -471,18 +492,19 @@
             pl.when(spill_out[kind])(lambda copy=spill(kind, q): copy.wait_send())
             if not last:
                 pl.when(halo_out[kind])(lambda copy=halo(kind, q): copy.wait_send())
-    for d in range(1, n_sub):
-        scatter_sub(d).wait_send()
-        gather("sub", d).wait_send()
-    for d in range(1, n_col):
-        scatter_col(d).wait_send()
-        gather("col", d).wait_send()
-    for d in range(1, n_row):
-        for cond, copy in (((row + d) % n_row < pieces, scatter_row(d)), (owns, gather("row", d))):
-            if pieces == n_row:
-                copy.wait_send()
-            else:
-                pl.when(cond)(lambda copy=copy: copy.wait_send())
+    for h in halves:
+        for d in range(1, n_sub):
+            scatter_sub(h, d).wait_send()
+            gather(h, "sub", d).wait_send()
+        for d in range(1, n_col):
+            scatter_col(h, d).wait_send()
+            gather(h, "col", d).wait_send()
+        for d in range(1, n_row):
+            for cond, copy in (((row + d) % n_row < pieces, scatter_row(h, d)), (owns, gather(h, "row", d))):
+                if pieces == n_row:
+                    copy.wait_send()
+                else:
+                    pl.when(cond)(lambda copy=copy: copy.wait_send())
 
 
 def solution(mesh):
@@ -492,11 +514,7 @@
         object_field, probe_field, patterns, offset_rows, offset_cols, counts, fresnel, object_step, probe_step
     ):
         n = probe_field.shape[1]
-        index = np.arange(n)
-        angles = 2.0 * np.pi / n * (index[:, None] * index[None, :] % n)
-        cosine = np.cos(angles).astype(np.float32)
-        sine = np.sin(angles).astype(np.float32)
-        sub_rows = n // n_sub
+        sub_rows = n // HALVES // n_sub
         col_rows = sub_rows // n_col
         row_rows = col_rows // min(n_row, col_rows // 8)
         f32 = jnp.float32
@@ -507,7 +525,8 @@
         region_shape = jax.ShapeDtypeStruct((2, 2 * n, 2 * n), f32)
         tile_shape = jax.ShapeDtypeStruct((2, n, n), f32)
         tile_scratch = pltpu.VMEM((2, n, n), f32)
-        limit = 24 * 1024 * 1024
+        limit = 28 * 1024 * 1024
+        cost = pl.CostEstimate(flops=6_000_000_000, bytes_accessed=8_000_000, transcendentals=0)
         copies = [dma((3, CHUNKS)), dma((3, CHUNKS))]
 
         region, left, right = pl.pallas_call(
@@ -515,15 +534,16 @@
             out_shape=(
                 region_shape,
                 jax.ShapeDtypeStruct((2 * n, 6 * n), jnp.bfloat16),
-                jax.ShapeDtypeStruct((6 * n, 2 * n), jnp.bfloat16),
+                jax.ShapeDtypeStruct((3 * n, 2 * n), jnp.bfloat16),
             ),
-            in_specs=[smem, vmem, vmem, vmem],
+            in_specs=[smem, vmem],
             out_specs=(vmem, vmem, vmem),
             scratch_shapes=copies,
+            cost_estimate=cost,
             compiler_params=pltpu.CompilerParams(
                 collective_id=0, has_side_effects=True, vmem_limit_bytes=limit
             ),
-        )(fresnel, object_field, jnp.asarray(cosine), jnp.asarray(sine))
+        )(fresnel, object_field)
 
         probe = probe_field
         for it in range(ITERS):
@@ -534,10 +554,11 @@
                 in_specs=[smem] * 3 + [vmem] * 5,
                 out_specs=(vmem, vmem),
                 scratch_shapes=[
-                    pltpu.VMEM((2, 3 * n, 2 * n), f32),
-                    pltpu.VMEM((6 * n, n), jnp.bfloat16),
-                    tile_scratch,
+                    pltpu.VMEM((2 * patterns.shape[0], 3 * n, 2 * n), f32),
+                    pltpu.VMEM((2 * patterns.shape[0], 6 * n, n), jnp.bfloat16),
+                    pltpu.VMEM((2 * patterns.shape[0], n, n), f32),
                 ],
+                cost_estimate=cost,
                 compiler_params=pltpu.CompilerParams(vmem_limit_bytes=limit),
             )(offset_rows, offset_cols, counts, region, probe, patterns, left, right)
             region, probe = pl.pallas_call(
@@ -548,17 +569,18 @@
                 scratch_shapes=[
                     tile_scratch,
                     tile_scratch,
-                    pltpu.VMEM((3, sub_rows, n), f32),
+                    pltpu.VMEM((HALVES, 3, sub_rows, n), f32),
                     tile_scratch,
                     tile_scratch,
                     tile_scratch,
-                    pltpu.VMEM((n_sub - 1, 3, sub_rows, n), f32),
-                    pltpu.VMEM((n_col - 1, 3, col_rows, n), f32),
-                    pltpu.VMEM((n_row - 1, 3, row_rows, n), f32),
+                    pltpu.VMEM((HALVES, n_sub - 1, 3, sub_rows, n), f32),
+                    pltpu.VMEM((HALVES, n_col - 1, 3, col_rows, n), f32),
+                    pltpu.VMEM((HALVES, n_row - 1, 3, row_rows, n), f32),
                 ]
                 + copies
                 + copies
-                + [dma((2, count - 1)) for count in (n_sub, n_sub, n_col, n_col, n_row, n_row)],
+                + [dma((HALVES, 2, count - 1)) for count in (n_sub, n_sub, n_col, n_col, n_row, n_row)],
+                cost_estimate=cost,
                 compiler_params=pltpu.CompilerParams(
                     collective_id=1 + it, has_side_effects=True, vmem_limit_bytes=limit
                 ),

time: 124 us -> 108 us (0.87)
  Pallas kernels: 112 us -> 101 us
  local copies, waits for them, and re-layouts: 8.02 us -> 2.64 us
    pallas_call x2, Pallas kernels: 28.1 us -> 22.6 us  [local(): pl.pallas_call(functools.partial(gradients, sizes), out_shape=(region_sha...]
    pallas_call x2, Pallas kernels: 65.8 us -> 60.4 us  [local(): pl.pallas_call(functools.partial(exchange_next, sizes, last), out_shape=(...]
    unnamed x24 -> x12, local copies, waits for them, and re-layouts: 8.02 us -> 2.64 us
where the time goes in v2:
time: 108 us; the launch traced here: 107 us
  Pallas kernels  101 us (94%)
  between operations  3.3 us (3%)
  local copies, waits for them, and re-layouts  2.64 us (2%)
    pallas_call x2, Pallas kernels, local(): pl.pallas_call(functools.partial(exchange_next, sizes, last), out_shape=(...  60.4 us
    pallas_call x2, Pallas kernels, local(): pl.pallas_call(functools.partial(gradients, sizes), out_shape=(region_sha...  22.6 us
    pallas_call x1, Pallas kernels, local(): pl.pallas_call(functools.partial(exchange_first, sizes), out_shape=(regio...  18.5 us
    unnamed x12, local copies, waits for them, and re-layouts  2.64 us

profile of v2, /device:TPU:0, one launch (start us, length us, event | category | flops | bytes accessed | tf_op | source)
XLA Modules:
  0.0 107.4 jit_solution(2462498553182357953)
XLA Ops:
  3.2 0.0 copy-start.1
  3.2 1.0 copy-done.1
  4.3 0.0 copy-start
  4.3 0.0 copy-start.2
  4.3 0.0 copy-start.3
  4.3 0.0 copy-start.4
  4.3 18.5 %shard_map.104 = (f32[2,512,512]{2,1,0:T(8,128)S(1)}, bf16[512,1536]{1,0:T(8,128)(2,1)S(1)}, bf16[768,512]{1,0:T(8,128)(2,1)S(1)}) custom-call(f32[1]{0:T(128)S(6)} %copy.14.fresnel_ref, f32[2,256,256]{2,1,0:T(8,128)S(1)} %copy-done.1), custom_call_target="tpu_custom_call" | custom-call | flops 6000000000 | bytes 8000000 | tf_op jit(solution)/shard_map/pallas_call | solution.py:532
  22.8 0.0 copy-done
  22.8 0.0 copy-done.2
  22.8 0.0 copy-done.3
  22.8 0.0 copy-done.4
  22.8 11.3 %shard_map.105 = (f32[2,512,512]{2,1,0:T(8,128)S(1)}, f32[3,256,256]{2,1,0:T(8,128)S(1)}) custom-call(s32[3]{0:T(128)S(1)} %copy-done.3, s32[3]{0:T(128)S(1)} %copy-done.4, s32[1]{0:T(128)S(6)} %copy.13.counts_ref, f32[2,512,512]{2,1,0:T(8,128)S(1)} %get-tuple-element.11.region.old_region, f32[2,256,256]{2,1,0:T(8,128)S(1)} %copy-done.2, ...), custom_call_target="tpu_custom_call" | custom-call | flops 6000000000 | bytes 8000000 | tf_op jit(solution)/shard_map/pallas_call | solution.py:551
  34.1 30.9 %shard_map.106 = (f32[2,512,512]{2,1,0:T(8,128)S(1)}, f32[2,256,256]{2,1,0:T(8,128)S(1)}) custom-call(f32[1]{0:T(128)S(6)} %copy.15.object_step_ref, f32[1]{0:T(128)S(6)} %copy.16.probe_step_ref, f32[2,512,512]{2,1,0:T(8,128)S(1)} %get-tuple-element.11.region.old_region, f32[2,256,256]{2,1,0:T(8,128)S(1)} %copy-done.2, ...), custom_call_target="tpu_custom_call" | custom-call | flops 6000000000 | bytes 8000000 | tf_op jit(solution)/shard_map/pallas_call | solution.py:564
  65.0 11.3 %shard_map.107 = (f32[2,512,512]{2,1,0:T(8,128)S(1)}, f32[3,256,256]{2,1,0:T(8,128)S(1)}) custom-call(s32[3]{0:T(128)S(1)} %copy-done.3, s32[3]{0:T(128)S(1)} %copy-done.4, s32[1]{0:T(128)S(6)} %copy.13.counts_ref, f32[2,512,512]{2,1,0:T(8,128)S(1)} %get-tuple-element.16.region.old_region, f32[2,256,256]{2,1,0:T(8,128)S(1)} %get-tuple-element.17.probe, ...), custom_call_target="tpu_custom_call" | custom-call | flops 6000000000 | bytes 8000000 | tf_op jit(solution)/shard_map/pallas_call | solution.py:551
  76.3 29.5 %shard_map.108 = (f32[2,256,256]{2,1,0:T(8,128)S(1)}, f32[2,256,256]{2,1,0:T(8,128)S(1)}) custom-call(f32[1]{0:T(128)S(6)} %copy.15.object_step_ref, f32[1]{0:T(128)S(6)} %copy.16.probe_step_ref, f32[2,512,512]{2,1,0:T(8,128)S(1)} %get-tuple-element.16.region.old_region, f32[2,256,256]{2,1,0:T(8,128)S(1)} %get-tuple-element.17.probe, ...), custom_call_target="tpu_custom_call" | custom-call | flops 6000000000 | bytes 8000000 | tf_op jit(solution)/shard_map/pallas_call | solution.py:564
  105.8 0.8 copy.17
  106.6 0.8 copy.18
Async XLA Ops:
  3.2 1.0 copy-start.1
  4.3 18.5 %copy-start = (f32[3,256,256]{2,1,0:T(8,128)S(1)}, f32[3,256,256]{2,1,0:T(8,128)}, u32[]{:S(2)}) copy-start(f32[3,256,256]{2,1,0:T(8,128)} %patterns_ref.3) | copy-start | bytes 2359300
  4.3 18.5 %copy-start.2 = (f32[2,256,256]{2,1,0:T(8,128)S(1)}, f32[2,256,256]{2,1,0:T(8,128)}, u32[]{:S(2)}) copy-start(f32[2,256,256]{2,1,0:T(8,128)} %probe.3) | copy-start | bytes 1572868
  4.3 18.5 %copy-start.3 = (s32[3]{0:T(128)S(1)}, s32[3]{0:T(128)}, u32[]{:S(2)}) copy-start(s32[3]{0:T(128)} %rows_ref.3) | copy-start | bytes 40
  4.3 18.6 %copy-start.4 = (s32[3]{0:T(128)S(1)}, s32[3]{0:T(128)}, u32[]{:S(2)}) copy-start(s32[3]{0:T(128)} %cols_ref.3) | copy-start | bytes 40
